TPU v7x, 128 devices: a whole 4x4x4 slice. The times are simulated.
128 devices in a mesh: dp: 8 (over z, core), feat: 16 (over y, x).
Axes of the slice: x: 4, y: 4, z: 4, core: 2. Of those that a mesh axis runs over, the one named last changes fastest.
Arguments:
- codes: bfloat16 [45056, 32768], P('dp', 'feat'), may hold values from -4 to 4
- scales: float32 [256, 45056], P('feat', 'dp'), may hold values from 0.25 to 4
- logit_weight: bfloat16 [32768], P('feat'), may hold values from -0.03125 to 0.03125
- probes: bfloat16 [32768, 128], P('feat'), may hold values from -5 to 5
Outputs:
- factor: float32 [32768, 128], P('feat', 'dp')
All inputs are finite; a program needn't handle non-finite values.
Results may differ from a plain program's by a relative error of at most 0.0004.
The roundings to bfloat16 on the way count: a program that leaves them out, or rounds other values in their place, can miss the bound.
Values sent between devices are 32-bit elements; how exact they have to be, the bound alone decides.
A program may use at most 192 MiB of HBM per device.

v0:
```python
import jax
import jax.numpy as jnp
from jax import lax
from jax.sharding import PartitionSpec as P

F = 32768
K = 128
QB = 128


def cut_along(shard, dim, size):
    lengths = shard.shape
    parts = shard.reshape(*lengths[:dim], size, lengths[dim] // size, *lengths[dim + 1 :])
    return jnp.moveaxis(parts, dim, 0)


def sum_at_owner(shard, axis, dim):
    parts = cut_along(shard, dim, lax.axis_size(axis))
    arrived = lax.all_to_all(parts, axis, split_axis=0, concat_axis=0, tiled=True)
    return arrived.sum(axis=0)


def from_everyone(shard, axis):
    copies = jnp.broadcast_to(shard, (lax.axis_size(axis), *shard.shape))
    return lax.all_to_all(copies, axis, split_axis=0, concat_axis=0, tiled=True)


def of_everyone(shard, axis):
    return from_everyone(shard, axis).sum(axis=0)


def together(arrays, axis):
    flat, at, gathered = (jnp.concatenate([a.reshape(-1) for a in arrays]), 0, [])
    so_far = of_everyone(flat, axis)
    for a in arrays:
        gathered.append(so_far[at : at + a.size].reshape(a.shape))
        at += a.size
    return tuple(gathered)


def laid_out(parts, dim):
    parts = jnp.moveaxis(parts, 0, dim)
    lengths = parts.shape
    return parts.reshape(*lengths[:dim], lengths[dim] * lengths[dim + 1], *lengths[dim + 2 :])


def gathered_copies(shard, axis, dim):
    return laid_out(from_everyone(shard, axis), dim)


def finish_gram(cross, self_gram, squares):
    shift = 0.1 * jnp.sqrt(squares / (F * K))
    gram = cross + shift * self_gram
    gram = 0.5 * (gram + gram.T)
    lower = jnp.linalg.cholesky(gram)
    inverse = lax.linalg.triangular_solve(
        lower, jnp.eye(K, dtype=jnp.float32), left_side=True, lower=True
    )
    return (shift, inverse)


def body(codes, scales, logit_weight, probes):
    rows = codes.shape[0]
    local_feat = codes.shape[1]
    blocks = local_feat // QB
    total = rows * lax.axis_size("dp")
    hi = lax.Precision.HIGHEST
    slab = (
        (codes.reshape(rows, blocks, QB).astype(jnp.float32) * scales.T[:, :, None])
        .reshape(rows, local_feat)
        .astype(jnp.bfloat16)
    )
    projected = jnp.dot(slab, probes, preferred_element_type=jnp.float32)
    logits = jnp.dot(slab, logit_weight, preferred_element_type=jnp.float32)
    projected, logits = lax.psum((projected, logits), "feat")
    prob = jax.nn.sigmoid(logits)
    curvature = prob * (1.0 - prob) / total
    tilted = (curvature[:, None] * projected).astype(jnp.bfloat16)
    partial_sketch = lax.dot_general(
        slab, tilted, (((0,), (0,)), ((), ())), preferred_element_type=jnp.float32
    )
    probe_full = probes.astype(jnp.float32)
    self_gram = jnp.dot(probe_full.T, probe_full, precision=hi)
    width = K // lax.axis_size("dp")
    first = lax.axis_index("dp") * width
    scale_out = jnp.sqrt(jnp.float32(F))
    sketch_cols = sum_at_owner(partial_sketch, "dp", 1)
    cross_cols = jnp.dot(probe_full.T, sketch_cols, precision=hi)
    squares = jnp.sum(sketch_cols * sketch_cols)
    cross_cols, self_gram, squares = together((cross_cols, self_gram, squares), "feat")
    cross = gathered_copies(cross_cols, "dp", 1)
    squares = of_everyone(squares, "dp")
    shift, inverse = finish_gram(cross, self_gram, squares)
    probe_cols = lax.dynamic_slice_in_dim(probe_full, first, width, 1)
    shifted_cols = sketch_cols + shift * probe_cols
    mine = lax.dynamic_slice_in_dim(inverse.T, first, width, 1)
    result = jnp.dot(gathered_copies(shifted_cols, "dp", 1), mine, precision=hi)
    return scale_out * result


def solution(mesh):
    placed = (P("dp", "feat"), P("feat", "dp"), P("feat"), P("feat", None))
    return jax.shard_map(
        body, mesh=mesh, in_specs=placed, out_specs=P("feat", "dp"), check_vma=False
    )
```

profile of v0, /device:TPU:1, one launch (start us, length us, event | category | flops | bytes accessed | tf_op | source)
XLA Modules:
  0.0 292.5 jit_solution(356774122993096932)
XLA Ops:
  6.5 0.0 copy-start
  6.5 0.0 all-reduce.2.cloned.1.call-start
  6.5 1.9 copy.33
  8.4 23.0 %mul.55 = f32[5632,16,128]{2,1,0:T(8,128)} broadcast(f32[5632,16]{1,0:T(8,128)S(1)} %copy.33), dimensions={0,1} | broadcast | bytes 46497792 | tf_op jit(solution)/shard_map/mul | solution.py:69
  31.4 31.3 %fusion = bf16[5632,2048]{1,0:T(8,128)(2,1)} fusion(f32[704,8,16,128]{3,2,1,0:T(8,128)} %bitcast.56, bf16[5632,2048]{1,0:T(8,128)(2,1)} %param.4), kind=kLoop, calls=%fused_computation.1 | loop fusion | flops 34603008 | bytes 92274688 | tf_op jit(solution)/shard_map/convert_element_type | solution.py:71
  62.7 0.0 copy-done
  62.7 0.0 copy-start.1
  62.7 12.4 %fusion.16 = f32[5632,128]{1,0:T(8,128)} fusion(bf16[5632,2048]{1,0:T(8,128)(2,1)} %fusion, bf16[2048,128]{1,0:T(8,128)(2,1)S(1)} %copy-done), kind=kOutput, calls=%fused_computation.34 | convolution fusion | flops 2952790016 | bytes 26476544 | tf_op jit(solution)/shard_map/dot_general | solution.py:73
  75.1 0.0 all-reduce.2.cloned.1.call-update
  75.1 0.0 copy-done.1
  75.1 10.7 %convolution_reduce_fusion = f32[5632]{0:T(1024)S(1)} fusion(bf16[5632,2048]{1,0:T(8,128)(2,1)} %fusion, bf16[2048,1]{0,1:T(2,128)(2,1)S(1)} %reshape.53), kind=kOutput, calls=%fused_computation.9 | convolution fusion | flops 23068672 | bytes 23095296 | tf_op jit(solution)/shard_map/dot_general | solution.py:74
  85.8 61.6 %psum.14 = f32[5632]{0:T(1024)S(1)} all-reduce(f32[5632]{0:T(1024)S(1)} %convolution_reduce_fusion), channel_id=1, replica_groups=mesh['dp'=8,'feat'=16] {'feat'}, use_global_device_ids=true, to_apply=%region_0.0 | all-reduce | flops 5632 | bytes 45056 | tf_op jit(solution)/shard_map/psum | solution.py:75
  147.4 24.7 %all-reduce.2.cloned.1.call-done = f32[5632,128]{1,0:T(8,128)} async-done(((f32[5632,128]{1,0:T(8,128)}), f32[5632,128]{1,0:T(8,128)}) %all-reduce.2.cloned.1.call-update) | async-done | bytes 2883600 | tf_op jit(solution)/shard_map/psum | solution.py:75
  172.2 3.7 %fusion.6 = bf16[128,5632]{0,1:T(8,128)(2,1)S(1)} fusion(f32[5632,128]{1,0:T(8,128)} %all-reduce.2.cloned.1.call-done, f32[5632]{0:T(1024)S(1)} %fusion.13), kind=kLoop, calls=%fused_computation.8 | loop fusion | flops 1441792 | bytes 4347904 | tf_op jit(solution)/shard_map/dot_general | solution.py:79
  175.9 0.7 copy.34
  176.6 10.2 %fusion.3 = f32[8,2048,16]{1,2,0:T(8,128)} fusion(bf16[8,16,5632]{2,1,0:T(8,128)(2,1)S(1)} %bitcast.58, bf16[5632,2048]{1,0:T(8,128)(2,1)} %fusion), kind=kOutput, calls=%fused_computation.5 | convolution fusion | flops 2952790016 | bytes 25559040 | tf_op jit(solution)/shard_map/dot_general | solution.py:79
  186.8 5.6 %all-to-all-start = ((f32[8,2048,16]{1,2,0:T(8,128)}), f32[8,2048,16]{1,2,0:T(8,128)S(1)}, u32[]{:S(2)}, u32[]{:S(2)}) async-start(f32[8,2048,16]{1,2,0:T(8,128)} %fusion.3), calls=%async_computation | async-start | bytes 2097152 | tf_op jit(solution)/shard_map/all_to_all | solution.py:19
  192.4 0.3 convolution_bitcast_fusion
  192.7 14.8 %all-to-all-done = f32[8,2048,16]{1,2,0:T(8,128)S(1)} async-done(((f32[8,2048,16]{1,2,0:T(8,128)}), f32[8,2048,16]{1,2,0:T(8,128)S(1)}, u32[]{:S(2)}, u32[]{:S(2)}) %all-to-all-start) | async-done | bytes 1048608 | tf_op jit(solution)/shard_map/all_to_all | solution.py:19
  207.5 0.1 reduce_sum.36
  207.6 0.3 convolution_bitcast_fusion.1
  207.9 0.6 multiply_reduce_fusion
  208.5 0.1 copy.35
  208.6 0.1 reshape.46
  208.7 0.7 pad_maximum_fusion
  209.4 1.6 broadcast_in_dim.16
  211.0 4.5 %all-to-all-start.1 = ((f32[16,1,18433]{2,1,0:T(1,128)}), f32[16,1,18433]{2,1,0:T(1,128)S(1)}, u32[]{:S(2)}, u32[]{:S(2)}) async-start(f32[16,1,18433]{2,1,0:T(1,128)} %broadcast_in_dim.16), calls=%async_computation.1 | async-start | bytes 2375680 | tf_op jit(solution)/shard_map/all_to_all | solution.py:25
  215.5 0.2 constant_dynamic-slice_fusion
  215.7 0.2 copy.48
  215.9 16.9 %all-to-all-done.1 = f32[16,1,18433]{2,1,0:T(1,128)S(1)} async-done(((f32[16,1,18433]{2,1,0:T(1,128)}), f32[16,1,18433]{2,1,0:T(1,128)S(1)}, u32[]{:S(2)}, u32[]{:S(2)}) %all-to-all-start.1) | async-done | bytes 1179744 | tf_op jit(solution)/shard_map/all_to_all | solution.py:25
  232.8 0.7 reduce_sum.38
  233.5 0.6 slice.22
  234.1 1.3 broadcast_in_dim.17
  235.4 6.2 %all-to-all-start.2 = ((f32[8,1,1]{2,1,0:T(1,128)}), f32[8,1,1]{2,1,0:T(1,128)S(1)}, u32[]{:S(2)}, u32[]{:S(2)}) async-start(f32[8,1,1]{2,1,0:T(1,128)} %broadcast_in_dim.17), calls=%async_computation.2 | async-start | bytes 8192 | tf_op jit(solution)/shard_map/all_to_all | solution.py:25
  241.6 0.1 reshape.51
  241.7 0.1 copy.39
  241.7 4.4 %all-to-all-done.2 = f32[8,1,1]{2,1,0:T(1,128)S(1)} async-done(((f32[8,1,1]{2,1,0:T(1,128)}), f32[8,1,1]{2,1,0:T(1,128)S(1)}, u32[]{:S(2)}, u32[]{:S(2)}) %all-to-all-start.2) | async-done | bytes 64 | tf_op jit(solution)/shard_map/all_to_all | solution.py:25
  246.1 0.6 broadcast_in_dim.19
  246.8 3.9 %all-to-all-start.4 = ((f32[8,128,16]{1,2,0:T(8,128)}), f32[8,128,16]{1,2,0:T(8,128)S(1)}, u32[]{:S(2)}, u32[]{:S(2)}) async-start(f32[8,128,16]{1,2,0:T(8,128)} %broadcast_in_dim.19), calls=%async_computation.4 | async-start | bytes 131072 | tf_op jit(solution)/shard_map/all_to_all | solution.py:25
  250.7 0.7 reduce_sum.39
  252.2 0.1 copy.40
  252.3 3.3 %all-to-all-done.4 = f32[8,128,16]{1,2,0:T(8,128)S(1)} async-done(((f32[8,128,16]{1,2,0:T(8,128)}), f32[8,128,16]{1,2,0:T(8,128)S(1)}, u32[]{:S(2)}, u32[]{:S(2)}) %all-to-all-start.4) | async-done | bytes 65568 | tf_op jit(solution)/shard_map/all_to_all | solution.py:25
  255.6 1.1 broadcast_in_dim.18
  256.7 4.2 %all-to-all-start.3 = ((f32[8,2048,16]{1,2,0:T(8,128)}), f32[8,2048,16]{1,2,0:T(8,128)S(1)}, u32[]{:S(2)}, u32[]{:S(2)}) async-start(f32[8,2048,16]{1,2,0:T(8,128)} %broadcast_in_dim.18), calls=%async_computation.3 | async-start | bytes 2097152 | tf_op jit(solution)/shard_map/all_to_all | solution.py:25
  260.9 0.1 copy.41
  261.0 0.1 copy.42
  261.1 11.7 %cholesky.14 = f32[128,128]{1,0:T(8,128)S(1)} custom-call(f32[128,128]{1,0:T(8,128)S(1)} %fusion.11), custom_call_target="Cholesky" | custom-call | tf_op jit(solution)/shard_map/jit(cholesky)/cholesky | solution.py:55
  272.9 0.6 compare_reduce_fusion
  273.5 0.7 fusion.7
  274.2 9.8 %custom-call.6 = f32[1,128,128]{1,2,0:T(8,128)S(1)} custom-call(f32[1,128,128]{2,1,0:T(8,128)S(1)} %fusion.7), custom_call_target="InvertDiagBlocksLowerTriangular" | custom-call | tf_op jit(solution)/shard_map/triangular_solve | solution.py:56
  284.0 0.2 fusion.9
  284.3 0.0 all-to-all-done.3
  284.3 1.3 convolution_multiply_fusion
  (9 shorter events, 0.1 us)
Async XLA Ops:
  6.5 56.2 %copy-start = (bf16[2048,128]{1,0:T(8,128)(2,1)S(1)}, bf16[2048,128]{1,0:T(8,128)(2,1)}, u32[]{:S(2)}) copy-start(bf16[2048,128]{1,0:T(8,128)(2,1)} %param.7) | copy-start | bytes 1572868
  6.5 165.6 %all-reduce.2.cloned.1.call-start = ((), (), s32[]{:S(2)}) async-start(), calls=%async_computation.5 | async-start | bytes 5767168 | tf_op jit(solution)/shard_map/psum | solution.py:75
  62.7 12.4 %copy-start.1 = (bf16[2048]{0:T(1024)(128)(2,1)S(1)}, bf16[2048]{0:T(1024)(128)(2,1)}, u32[]{:S(2)}) copy-start(bf16[2048]{0:T(1024)(128)(2,1)} %param.6) | copy-start | bytes 12292
  186.8 20.7 %all-to-all-start = ((f32[8,2048,16]{1,2,0:T(8,128)}), f32[8,2048,16]{1,2,0:T(8,128)S(1)}, u32[]{:S(2)}, u32[]{:S(2)}) async-start(f32[8,2048,16]{1,2,0:T(8,128)} %fusion.3), calls=%async_computation | async-start | bytes 2097152 | tf_op jit(solution)/shard_map/all_to_all | solution.py:19
  211.0 21.8 %all-to-all-start.1 = ((f32[16,1,18433]{2,1,0:T(1,128)}), f32[16,1,18433]{2,1,0:T(1,128)S(1)}, u32[]{:S(2)}, u32[]{:S(2)}) async-start(f32[16,1,18433]{2,1,0:T(1,128)} %broadcast_in_dim.16), calls=%async_computation.1 | async-start | bytes 2375680 | tf_op jit(solution)/shard_map/all_to_all | solution.py:25
  235.4 10.7 %all-to-all-start.2 = ((f32[8,1,1]{2,1,0:T(1,128)}), f32[8,1,1]{2,1,0:T(1,128)S(1)}, u32[]{:S(2)}, u32[]{:S(2)}) async-start(f32[8,1,1]{2,1,0:T(1,128)} %broadcast_in_dim.17), calls=%async_computation.2 | async-start | bytes 8192 | tf_op jit(solution)/shard_map/all_to_all | solution.py:25
  246.8 8.8 %all-to-all-start.4 = ((f32[8,128,16]{1,2,0:T(8,128)}), f32[8,128,16]{1,2,0:T(8,128)S(1)}, u32[]{:S(2)}, u32[]{:S(2)}) async-start(f32[8,128,16]{1,2,0:T(8,128)} %broadcast_in_dim.19), calls=%async_computation.4 | async-start | bytes 131072 | tf_op jit(solution)/shard_map/all_to_all | solution.py:25
  256.7 27.6 %all-to-all-start.3 = ((f32[8,2048,16]{1,2,0:T(8,128)}), f32[8,2048,16]{1,2,0:T(8,128)S(1)}, u32[]{:S(2)}, u32[]{:S(2)}) async-start(f32[8,2048,16]{1,2,0:T(8,128)} %broadcast_in_dim.18), calls=%async_computation.3 | async-start | bytes 2097152 | tf_op jit(solution)/shard_map/all_to_all | solution.py:25
Sparse Core Ops, SparseCore 0:
  75.2 96.8 all-reduce.1
where the time goes:
time: 293 us; the launch traced here: 292 us
  waiting for transfers between devices  64.1 us (22%)
  blocking collectives  61.6 us (21%)
  other arithmetic  60.7 us (21%)
  matrix products  35.5 us (12%)
  local copies, waits for them, and re-layouts  31.8 us (11%)
  starting transfers between devices  24.4 us (8%)
  between operations  14.3 us (5%)
    psum x1, blocking collectives, body(): projected, logits = lax.psum((projected, logits), 'feat')  61.6 us
    convert_element_type x1, other arithmetic, body(): slab = (codes.reshape(rows, blocks, QB).astype(jnp.float32) * scales.T[:,...  31.3 us
    psum x1, waiting for transfers between devices, body(): projected, logits = lax.psum((projected, logits), 'feat')  24.7 us
    all_to_all x4, waiting for transfers between devices, from_everyone(): return lax.all_to_all(copies, axis, split_axis=0, concat_axis=0, tiled=True)  24.6 us
    mul x1, local copies, waits for them, and re-layouts, body(): codes.reshape(rows, blocks, QB).astype(jnp.float32) * scales.T[:, :, None]  23 us
    all_to_all x4, starting transfers between devices, from_everyone(): return lax.all_to_all(copies, axis, split_axis=0, concat_axis=0, tiled=True)  18.9 us
    all_to_all x1, waiting for transfers between devices, sum_at_owner(): lax.all_to_all(parts, axis, split_axis=0, concat_axis=0, tiled=True)  14.8 us
    another operation x3, other arithmetic, finish_gram(): lower = jnp.linalg.cholesky(gram)  12.4 us
  transfers between devices with their start and end apart: 6, of which 5 were waited for; matrix products, arithmetic and copies ran while one was open for 12% of the time, Pallas kernels for 0%

commit v1 on v0

v1 whole, which is shorter than its diff:
```python
import functools

import jax
import jax.numpy as jnp
from jax import lax
from jax.experimental import pallas as pl
from jax.experimental.pallas import tpu as pltpu
from jax.sharding import PartitionSpec as P

F = 32768
K = 128
QB = 128
ROWS = 5632
COLS = 2048
BLOCKS = COLS // QB
CHUNK = 512
STEPS = ROWS // CHUNK
LAG = 2
HALF = CHUNK // 2
PA = HALF // 4
PB = PA // 4
MESH = pl.DeviceIdType.MESH
HI = lax.Precision.HIGHEST
F32 = jnp.float32
BF16 = jnp.bfloat16


def wait_for(ref, sem):
    pltpu.make_async_copy(ref, ref, sem).wait()


def lower_inverse(g_ref, w_ref, gram):
    sub = lax.broadcasted_iota(jnp.int32, (K, K), 0)
    lane = lax.broadcasted_iota(jnp.int32, (K, K), 1)
    g_ref[...] = gram
    w_ref[...] = jnp.where(sub == lane, 1.0, 0.0).astype(F32)

    def step(k, _):
        a = g_ref[...]
        w = w_ref[...]
        row_a = g_ref[pl.ds(k, 1), :]
        row_w = w_ref[pl.ds(k, 1), :]
        col = jnp.sum(jnp.where(lane == k, a, 0.0), axis=1, keepdims=True)
        pivot = jnp.sum(
            jnp.where(lane[:1] == k, row_a, 0.0), axis=1, keepdims=True
        )
        factor = jnp.where(sub[:, :1] > k, col / pivot, 0.0)
        g_ref[...] = a - factor * row_a
        w_ref[...] = w - factor * row_w
        return 0

    lax.fori_loop(0, K, step, 0)
    diag = jnp.sum(jnp.where(sub == lane, g_ref[...], 0.0), axis=1, keepdims=True)
    w_ref[...] = w_ref[...] * lax.rsqrt(diag)


def kernel(
    codes, scales, pext, out,
    slab, part, ra, sa, rb, tilt, own_p, own_t,
    lg, lx, ly, acc, rc, rz, full,
    gsend, g1, g3, gf, sq1, sq2, gmat, wmat,
    code_sem, send_sem, recv_sem, lsend_sem, lrecv_sem, tsend, trecv,
):
    d = lax.axis_index("dp")
    f = lax.axis_index("feat")
    z, core = d // 2, d % 2
    y, x = f // 4, f % 4

    def rows_at(c, off, size):
        return pl.ds(pl.multiple_of(c * CHUNK + off, 8), size)

    def code_copy(c):
        at = pl.ds(c * CHUNK, CHUNK)
        return pltpu.make_async_copy(codes.at[at], slab.at[at], code_sem.at[c])

    for c in range(STEPS):
        code_copy(c).start()

    def x_peer(j):
        return (d, y * 4 + (x + j) % 4)

    def y_peer(j):
        return (d, ((y + j) % 4) * 4 + x)

    def plane_peer(j):
        return (d, (f + j) % 16)

    def dp_peer(j):
        return ((d + j) % 8, f)

    def z_peer(j):
        return (((z + j) % 4) * 2 + core, f)

    core_peer = (z * 2 + 1 - core, f)
    barrier = pltpu.get_barrier_semaphore()
    for j in range(1, 16):
        pl.semaphore_signal(barrier, 1, device_id=plane_peer(j), device_id_type=MESH)
    for j in range(1, 8):
        pl.semaphore_signal(barrier, 1, device_id=dp_peer(j), device_id_type=MESH)
    pl.semaphore_wait(barrier, 22)

    axes = ((x, y, x_peer, y_peer), (y, x, y_peer, x_peer))

    def send(src, dst, ssem, rsem, peer):
        pltpu.make_async_remote_copy(
            src, dst, ssem, rsem, device_id=peer, device_id_type=MESH
        ).start()

    acc[...] = jnp.zeros_like(acc)
    lg[...] = jnp.zeros_like(lg)
    eye = lax.broadcasted_iota(jnp.int32, (K, K), 0) == lax.broadcasted_iota(
        jnp.int32, (K, K), 1
    )

    def stage_a(c):
        slot = c % (LAG + 1)
        pltpu.make_async_copy(
            codes.at[rows_at(c, 0, CHUNK)], slab.at[rows_at(c, 0, CHUNK)], code_sem.at[c]
        ).wait()

        def scale_rows(t, _):
            at = pl.ds(pl.multiple_of(c * CHUNK + t * 128, 128), 128)
            s = scales[:, at].T
            for b in range(BLOCKS):
                cols = pl.ds(b * QB, QB)
                v = slab[at, cols].astype(F32) * s[:, b : b + 1]
                slab[at, cols] = v.astype(BF16)
            return 0

        lax.fori_loop(0, CHUNK // 128, scale_rows, 0)
        rows = rows_at(c, 0, CHUNK)
        r = jnp.dot(slab[rows, :], pext[...], preferred_element_type=F32)
        part[rows, :] = r[:, :K]
        for t in range(CHUNK // 128):
            lg[c, t : t + 1, :] = jnp.sum(
                jnp.where(eye, r[t * 128 : (t + 1) * 128, K:], 0.0),
                axis=0, keepdims=True,
            )
        for j in range(1, 4):
            send(lg.at[c], lx.at[c, j - 1], lsend_sem.at[0, slot], lrecv_sem.at[0, c], x_peer(j))
        for h in range(2):
            pa, pb, a_peer, b_peer = axes[h]
            for j in (2, 1, 3):
                at = rows_at(c, h * HALF + ((pa + j) % 4) * PA, PA)
                send(part.at[at], ra.at[h, c, j - 1], send_sem.at[0, h, slot], recv_sem.at[0, h, c], a_peer(j))

    def stage_b(c):
        slot = c % (LAG + 1)
        wait_for(lx.at[c], lrecv_sem.at[0, c])
        wait_for(lx.at[c], lsend_sem.at[0, slot])
        lg[c] = lg[c] + lx[c, 0] + lx[c, 1] + lx[c, 2]
        for j in range(1, 4):
            send(lg.at[c], ly.at[c, j - 1], lsend_sem.at[1, slot], lrecv_sem.at[1, c], y_peer(j))
        for h in range(2):
            pa, pb, a_peer, b_peer = axes[h]
            wait_for(ra.at[h, c], recv_sem.at[0, h, c])
            wait_for(ra.at[h, c], send_sem.at[0, h, slot])
            at = rows_at(c, h * HALF + pa * PA, PA)
            sa[h, c] = part[at, :] + ra[h, c, 0] + ra[h, c, 1] + ra[h, c, 2]
            for j in (2, 1, 3):
                at = pl.ds(pl.multiple_of(((pb + j) % 4) * PB, 8), PB)
                send(sa.at[h, c, at], rb.at[h, c, j - 1], send_sem.at[1, h, slot], recv_sem.at[1, h, c], b_peer(j))

    def stage_c(c):
        slot = c % (LAG + 1)
        wait_for(ly.at[c], lrecv_sem.at[1, c])
        wait_for(ly.at[c], lsend_sem.at[1, slot])
        logits = lg[c] + ly[c, 0] + ly[c, 1] + ly[c, 2]
        s = 1.0 / (1.0 + jnp.exp(-logits))
        lg[c] = s * (1.0 - s) / 45056.0
        lane = lax.broadcasted_iota(jnp.int32, (PB, K), 1)
        sub = lax.broadcasted_iota(jnp.int32, (PB, K), 0)
        for h in range(2):
            pa, pb, a_peer, b_peer = axes[h]
            wait_for(rb.at[h, c], recv_sem.at[1, h, c])
            wait_for(rb.at[h, c], send_sem.at[1, h, slot])
            at = pl.ds(pl.multiple_of(pb * PB, 8), PB)
            p = sa[h, c, at, :] + rb[h, c, 0] + rb[h, c, 1] + rb[h, c, 2]
            curv = lg[c, pl.ds(h * 2 + pa // 2, 1), :]
            first = (pa % 2) * PA + pb * PB
            column = jnp.sum(
                jnp.where(lane == sub + first, curv, 0.0), axis=1, keepdims=True
            )
            t = (column * p).astype(BF16).astype(F32)
            mine = rows_at(c, h * HALF + pa * PA + pb * PB, PB)
            tilt[mine, :] = t
            keep = pl.ds(pl.multiple_of((c * 2 + h) * PB, 8), PB)
            own_p[keep, :] = p
            own_t[keep, :] = t
            for j in (2, 1, 3):
                send(tilt.at[mine], tilt.at[mine], send_sem.at[2, h, slot], recv_sem.at[2, h, c], b_peer(j))

    def stage_d(c):
        slot = c % (LAG + 1)
        for h in range(2):
            pa, pb, a_peer, b_peer = axes[h]
            wait_for(tilt.at[pl.ds(0, 3 * PB)], recv_sem.at[2, h, c])
            wait_for(tilt.at[pl.ds(0, 3 * PB)], send_sem.at[2, h, slot])
            mine = rows_at(c, h * HALF + pa * PA, PA)
            for j in (2, 1, 3):
                send(tilt.at[mine], tilt.at[mine], send_sem.at[3, h, slot], recv_sem.at[3, h, c], a_peer(j))

    def stage_e(c):
        slot = c % (LAG + 1)
        for h in range(2):
            wait_for(tilt.at[pl.ds(0, 3 * PA)], recv_sem.at[3, h, c])
            wait_for(tilt.at[pl.ds(0, 3 * PA)], send_sem.at[3, h, slot])
        rows = rows_at(c, 0, CHUNK)
        t = tilt[rows, :].T.astype(BF16)
        for p in range(8):
            acc[p] += jnp.dot(t, slab[rows, p * 256 : (p + 1) * 256], preferred_element_type=F32)

    def gram_out():
        cross = lax.dot_general(
            own_p[...], own_t[...], (((0,), (0,)), ((), ())),
            precision=HI, preferred_element_type=F32,
        )
        probes = pext[:, :K]
        selfg = lax.dot_general(
            probes, probes, (((0,), (0,)), ((), ())), preferred_element_type=F32
        ) * 0.125
        for i in range(16):
            gsend[i, :8] = cross[i * 8 : (i + 1) * 8]
            gsend[i, 8:] = selfg[i * 8 : (i + 1) * 8]
        for j in range(1, 16):
            send(gsend.at[(f + j) % 16], g1.at[f], tsend.at[0], trecv.at[0], plane_peer(j))

    def tick(t, _):
        def at_lag(n, stage):
            c = t - n * LAG

            @pl.when((c >= 0) & (c < STEPS))
            def _():
                stage(c)

        at_lag(3, stage_d)
        at_lag(2, stage_c)
        at_lag(1, stage_b)
        at_lag(0, stage_a)

        @pl.when(t == STEPS + 2 * LAG)
        def _():
            gram_out()

        at_lag(4, stage_e)
        return 0

    lax.fori_loop(0, STEPS + 4 * LAG, tick, 0)

    theirs = pl.ds((1 - core) * 4, 4)
    ours = core * 4
    send(acc.at[theirs], rc, tsend.at[1], trecv.at[1], core_peer)

    wait_for(g1.at[pl.ds(0, 15)], trecv.at[0])
    wait_for(g1.at[pl.ds(0, 15)], tsend.at[0])
    g1[f] = gsend[f]
    g = g1[0]
    for i in range(1, 16):
        g = g + g1[i]
    g3[d] = g
    for j in range(1, 8):
        send(g3.at[d], g3.at[d], tsend.at[2], trecv.at[2], dp_peer(j))

    wait_for(rc, trecv.at[1])
    wait_for(rc, tsend.at[1])
    for i in range(4):
        rc[i] = rc[i] + acc[ours + i]
    for j in (2, 1, 3):
        send(rc.at[(z + j) % 4], rz.at[j - 1], tsend.at[3], trecv.at[3], z_peer(j))

    wait_for(g3.at[pl.ds(0, 7)], trecv.at[2])
    wait_for(g3.at[pl.ds(0, 7)], tsend.at[2])
    g = g3[0]
    for i in range(1, 8):
        g = g + g3[i]
    gf[f] = g
    for j in range(1, 16):
        send(gf.at[f], gf.at[f], tsend.at[4], trecv.at[4], plane_peer(j))

    wait_for(rz, trecv.at[3])
    wait_for(rz, tsend.at[3])
    s = rc[z] + rz[0] + rz[1] + rz[2]
    mine = ours + z
    full[mine] = s
    sq = s * s
    sq = jnp.sum(sq.reshape(16, 8, 256), axis=0)
    sq1[d] = sq[:, :128] + sq[:, 128:]
    for j in range(1, 8):
        send(sq1.at[d], sq1.at[d], tsend.at[5], trecv.at[5], dp_peer(j))
    for j in (2, 1, 3):
        send(full.at[mine], full.at[mine], tsend.at[6], trecv.at[6], z_peer(j))

    wait_for(sq1.at[pl.ds(0, 7)], trecv.at[5])
    wait_for(sq1.at[pl.ds(0, 7)], tsend.at[5])
    sq = sq1[0]
    for i in range(1, 8):
        sq = sq + sq1[i]
    sq2[f] = sq
    for j in range(1, 16):
        send(sq2.at[f], sq2.at[f], tsend.at[7], trecv.at[7], plane_peer(j))

    wait_for(full.at[pl.ds(0, 3)], trecv.at[6])
    wait_for(full.at[pl.ds(0, 3)], tsend.at[6])
    send(full.at[pl.ds(ours, 4)], full.at[pl.ds(ours, 4)], tsend.at[8], trecv.at[8], core_peer)

    wait_for(gf.at[pl.ds(0, 15)], trecv.at[4])
    wait_for(gf.at[pl.ds(0, 15)], tsend.at[4])
    cross = jnp.concatenate([gf[i, :8] for i in range(16)], axis=0)
    selfg = jnp.concatenate([gf[i, 8:] for i in range(16)], axis=0)

    wait_for(sq2.at[pl.ds(0, 15)], trecv.at[7])
    wait_for(sq2.at[pl.ds(0, 15)], tsend.at[7])
    sq = sq2[0]
    for i in range(1, 16):
        sq = sq + sq2[i]
    total = jnp.sum(jnp.sum(sq, axis=1, keepdims=True), axis=0, keepdims=True)
    shift = 0.1 * jnp.sqrt(total / (F * K))
    gram = cross + shift * selfg
    gram = 0.5 * (gram + gram.T)
    lower_inverse(gmat, wmat, gram)
    inv = wmat[pl.ds(pl.multiple_of(d * 16, 8), 16), :] * (float(F) ** 0.5)
    from_probes = lax.dot_general(
        inv, pext[:, :K].astype(F32), (((1,), (1,)), ((), ())),
        precision=HI, preferred_element_type=F32,
    )

    wait_for(full.at[pl.ds(0, 4)], trecv.at[8])
    wait_for(full.at[pl.ds(0, 4)], tsend.at[8])
    for p in range(8):
        cols = slice(p * 256, (p + 1) * 256)
        out[:, cols] = shift * from_probes[:, cols] + jnp.dot(
            inv, full[p], precision=HI, preferred_element_type=F32
        )


def body(codes, scales, logit_weight, probes):
    pext = jnp.concatenate(
        [probes, jnp.broadcast_to(logit_weight[:, None], (COLS, K))], axis=1
    )
    vmem = pl.BlockSpec(memory_space=pltpu.VMEM)
    dma = pltpu.SemaphoreType.DMA
    result = pl.pallas_call(
        kernel,
        out_shape=jax.ShapeDtypeStruct((16, COLS), F32),
        in_specs=[pl.BlockSpec(memory_space=pl.ANY), vmem, vmem],
        out_specs=vmem,
        scratch_shapes=[
            pltpu.VMEM((ROWS, COLS), BF16),
            pltpu.VMEM((ROWS, K), F32),
            pltpu.VMEM((2, STEPS, 3, PA, K), F32),
            pltpu.VMEM((2, STEPS, PA, K), F32),
            pltpu.VMEM((2, STEPS, 3, PB, K), F32),
            pltpu.VMEM((ROWS, K), F32),
            pltpu.VMEM((ROWS // 16, K), F32),
            pltpu.VMEM((ROWS // 16, K), F32),
            pltpu.VMEM((STEPS, 8, K), F32),
            pltpu.VMEM((STEPS, 3, 8, K), F32),
            pltpu.VMEM((STEPS, 3, 8, K), F32),
            pltpu.VMEM((8, K, 256), F32),
            pltpu.VMEM((4, K, 256), F32),
            pltpu.VMEM((3, K, 256), F32),
            pltpu.VMEM((8, K, 256), F32),
            pltpu.VMEM((16, 16, K), F32),
            pltpu.VMEM((16, 16, K), F32),
            pltpu.VMEM((8, 16, K), F32),
            pltpu.VMEM((16, 16, K), F32),
            pltpu.VMEM((8, 8, K), F32),
            pltpu.VMEM((16, 8, K), F32),
            pltpu.VMEM((K, K), F32),
            pltpu.VMEM((K, K), F32),
            dma((STEPS,)),
            dma((4, 2, LAG + 1)),
            dma((4, 2, STEPS)),
            dma((2, LAG + 1)),
            dma((2, STEPS)),
            dma((9,)),
            dma((9,)),
        ],
        compiler_params=pltpu.CompilerParams(
            collective_id=0, has_side_effects=True, vmem_limit_bytes=58 << 20
        ),
        name="sketch",
    )(codes, scales, pext)
    return result.T


def solution(mesh):
    placed = (P("dp", "feat"), P("feat", "dp"), P("feat"), P("feat", None))
    return jax.shard_map(
        body, mesh=mesh, in_specs=placed, out_specs=P("feat", "dp"), check_vma=False
    )
```

time: 293 us -> 106 us (0.36)
  Pallas kernels: 0 us -> 101 us
  waiting for transfers between devices: 64.1 us -> 0 us
  blocking collectives: 61.6 us -> 0 us
  other arithmetic: 60.7 us -> 2.15 us
  matrix products: 35.5 us -> 0 us
  local copies, waits for them, and re-layouts: 31.8 us -> 2.59 us
  starting transfers between devices: 24.4 us -> 0 us
  between operations: 14.3 us -> 0.02 us
    pallas_call x0 -> x1, Pallas kernels: none -> 101 us  [body(): pl.pallas_call(kernel, out_shape=jax.ShapeDtypeStruct((16, COLS), F32), i...]
    psum x1 -> x0, blocking collectives: 61.6 us -> none  [body(): projected, logits = lax.psum((projected, logits), 'feat')]
    all_to_all x5 -> x0, waiting for transfers between devices: 39.3 us -> none  [the longest x4 24.6 us: from_everyone(): return lax.all_to_all(copies, axis, split_axis=0, concat_axis=0, tiled=True)]
    dot_general x6 -> x0, matrix products: 35.3 us -> none  [the longest x1 12.4 us: body(): projected = jnp.dot(slab, probes, preferred_element_type=jnp.float32)]
    convert_element_type x1 -> x0, other arithmetic: 31.3 us -> none  [body(): slab = (codes.reshape(rows, blocks, QB).astype(jnp.float32) * scales.T[:,...]
    psum x1 -> x0, waiting for transfers between devices: 24.7 us -> none  [body(): projected, logits = lax.psum((projected, logits), 'feat')]
    all_to_all x5 -> x0, starting transfers between devices: 24.4 us -> none  [the longest x4 18.9 us: from_everyone(): return lax.all_to_all(copies, axis, split_axis=0, concat_axis=0, tiled=True)]
    mul x3 -> x0, local copies, waits for them, and re-layouts: 23.2 us -> none  [the longest x1 23 us: body(): codes.reshape(rows, blocks, QB).astype(jnp.float32) * scales.T[:, :, None]]
  transfers between devices with their start and end apart: 6 -> 0, of which waited for: 5 -> 0; matrix products, arithmetic and copies ran while one was open for 12% -> 0% of each run, Pallas kernels for 0% -> 0%
where the time goes in v1:
time: 106 us
  Pallas kernels  101 us (95%)
  local copies, waits for them, and re-layouts  2.59 us (2%)
  other arithmetic  2.15 us (2%)
    pallas_call x1, Pallas kernels, body(): pl.pallas_call(kernel, out_shape=jax.ShapeDtypeStruct((16, COLS), F32), i...  101 us
    concatenate x1, other arithmetic, body(): jnp.concatenate([probes, jnp.broadcast_to(logit_weight[:, None], (COLS, K...  2.15 us

profile of v1, /device:TPU:1, one launch (start us, length us, event | category | flops | bytes accessed | tf_op | source)
XLA Modules:
  0.0 105.7 jit_solution(3823732500336580232)
XLA Ops:
  0.0 1.0 broadcast_in_dim.2
  1.0 2.1 %pad_maximum_fusion.pext = bf16[2048,256]{1,0:T(8,128)(2,1)} fusion(bf16[2048,128]{1,0:T(8,128)(2,1)S(1)} %broadcast_in_dim.2, bf16[2048,128]{1,0:T(8,128)(2,1)} %param.7), kind=kLoop, calls=%fused_computation | loop fusion | flops 2097152 | bytes 2097152 | tf_op jit(solution)/shard_map/concatenate | solution.py:337
  3.2 100.9 %sketch.1 = f32[16,2048]{1,0:T(8,128)} custom-call(bf16[5632,2048]{1,0:T(8,128)(2,1)} %codes.1, f32[16,5632]{1,0:T(8,128)} %scales.1, bf16[2048,256]{1,0:T(8,128)(2,1)} %pad_maximum_fusion.pext), custom_call_target="tpu_custom_call" | custom-call | tf_op jit(solution)/shard_map/sketch/pallas_call | solution.py:342
  104.1 1.6 %copy.6 = f32[2048,16]{0,1:T(8,128)} copy(f32[2048,16]{0,1:T(8,128)} %bitcast.1) | data formatting | bytes 262144

commit v2 on v1

--- a/solution.py
+++ b/solution.py
@@ -15,10 +15,13 @@
 BLOCKS = COLS // QB
 CHUNK = 512
 STEPS = ROWS // CHUNK
-LAG = 2
+LAG = 3
 HALF = CHUNK // 2
 PA = HALF // 4
 PB = PA // 4
+SPREAD = 256
+PANEL = 4
+STAGES = 3
 MESH = pl.DeviceIdType.MESH
 HI = lax.Precision.HIGHEST
 F32 = jnp.float32
@@ -34,32 +37,52 @@
     lane = lax.broadcasted_iota(jnp.int32, (K, K), 1)
     g_ref[...] = gram
     w_ref[...] = jnp.where(sub == lane, 1.0, 0.0).astype(F32)
-
-    def step(k, _):
+    lane_row, sub_col = lane[:1], sub[:, :1]
+
+    def step(i, _):
+        first = i * PANEL
         a = g_ref[...]
         w = w_ref[...]
-        row_a = g_ref[pl.ds(k, 1), :]
-        row_w = w_ref[pl.ds(k, 1), :]
-        col = jnp.sum(jnp.where(lane == k, a, 0.0), axis=1, keepdims=True)
-        pivot = jnp.sum(
-            jnp.where(lane[:1] == k, row_a, 0.0), axis=1, keepdims=True
-        )
-        factor = jnp.where(sub[:, :1] > k, col / pivot, 0.0)
-        g_ref[...] = a - factor * row_a
-        w_ref[...] = w - factor * row_w
+        row_a = [g_ref[pl.ds(first + j, 1), :] for j in range(PANEL)]
+        row_w = [w_ref[pl.ds(first + j, 1), :] for j in range(PANEL)]
+        col = [
+            jnp.sum(jnp.where(lane == first + j, a, 0.0), axis=1, keepdims=True)
+            for j in range(PANEL)
+        ]
+        corner = {
+            (m, j): jnp.sum(
+                jnp.where(lane_row == first + j, row_a[m], 0.0), axis=1, keepdims=True
+            )
+            for m in range(PANEL)
+            for j in range(m, PANEL)
+        }
+        for m in range(PANEL):
+            inverse = 1.0 / corner[m, m]
+            for j in range(m + 1, PANEL):
+                ratio = corner[m, j] * inverse
+                row_a[j] = row_a[j] - ratio * row_a[m]
+                row_w[j] = row_w[j] - ratio * row_w[m]
+                col[j] = col[j] - ratio * col[m]
+                for q in range(j, PANEL):
+                    corner[j, q] = corner[j, q] - ratio * corner[m, q]
+            factor = jnp.where(sub_col > first + m, col[m] * inverse, 0.0)
+            a = a - factor * row_a[m]
+            w = w - factor * row_w[m]
+        g_ref[...] = a
+        w_ref[...] = w
         return 0
 
-    lax.fori_loop(0, K, step, 0)
+    lax.fori_loop(0, K // PANEL, step, 0)
     diag = jnp.sum(jnp.where(sub == lane, g_ref[...], 0.0), axis=1, keepdims=True)
     w_ref[...] = w_ref[...] * lax.rsqrt(diag)
 
 
 def kernel(
-    codes, scales, pext, out,
-    slab, part, ra, sa, rb, tilt, own_p, own_t,
+    codes, scales, weight, probes, out,
+    pext, select, probes_t, held, slab, part, ra, sa, rb, tilt, own_p, own_t,
     lg, lx, ly, acc, rc, rz, full,
     gsend, g1, g3, gf, sq1, sq2, gmat, wmat,
-    code_sem, send_sem, recv_sem, lsend_sem, lrecv_sem, tsend, trecv,
+    code_sem, send_sem, recv_sem, lsend_sem, lrecv_sem, tsend, trecv, csend, crecv,
 ):
     d = lax.axis_index("dp")
     f = lax.axis_index("feat")
@@ -70,10 +93,11 @@
         return pl.ds(pl.multiple_of(c * CHUNK + off, 8), size)
 
     def code_copy(c):
-        at = pl.ds(c * CHUNK, CHUNK)
-        return pltpu.make_async_copy(codes.at[at], slab.at[at], code_sem.at[c])
-
-    for c in range(STEPS):
+        return pltpu.make_async_copy(
+            codes.at[rows_at(c, 0, CHUNK)], held.at[c % STAGES], code_sem.at[c % STAGES]
+        )
+
+    for c in range(STAGES):
         code_copy(c).start()
 
     def x_peer(j):
@@ -97,6 +121,13 @@
         pl.semaphore_signal(barrier, 1, device_id=plane_peer(j), device_id_type=MESH)
     for j in range(1, 8):
         pl.semaphore_signal(barrier, 1, device_id=dp_peer(j), device_id_type=MESH)
+    pext[:, :K] = probes[...]
+    block = lax.broadcasted_iota(jnp.int32, (3 * BLOCKS, COLS), 0) % BLOCKS
+    lane_block = lax.broadcasted_iota(jnp.int32, (3 * BLOCKS, COLS), 1) // QB
+    select[...] = jnp.where(block == lane_block, 1.0, 0.0).astype(BF16)
+    for b in range(BLOCKS):
+        row = weight[...].astype(F32)[b : b + 1]
+        pext[b * QB : (b + 1) * QB, K:] = jnp.broadcast_to(row, (K, QB)).T.astype(BF16)
     pl.semaphore_wait(barrier, 22)
 
     axes = ((x, y, x_peer, y_peer), (y, x, y_peer, x_peer))
@@ -114,21 +145,25 @@
 
     def stage_a(c):
         slot = c % (LAG + 1)
-        pltpu.make_async_copy(
-            codes.at[rows_at(c, 0, CHUNK)], slab.at[rows_at(c, 0, CHUNK)], code_sem.at[c]
-        ).wait()
-
-        def scale_rows(t, _):
-            at = pl.ds(pl.multiple_of(c * CHUNK + t * 128, 128), 128)
-            s = scales[:, at].T
-            for b in range(BLOCKS):
-                cols = pl.ds(b * QB, QB)
-                v = slab[at, cols].astype(F32) * s[:, b : b + 1]
-                slab[at, cols] = v.astype(BF16)
-            return 0
-
-        lax.fori_loop(0, CHUNK // 128, scale_rows, 0)
+        code_copy(c).wait()
+
         rows = rows_at(c, 0, CHUNK)
+        rest = scales[:, pl.ds(pl.multiple_of(c * CHUNK, 128), CHUNK)]
+        thirds = []
+        for _ in range(3):
+            thirds.append(rest.astype(BF16).astype(F32))
+            rest = rest - thirds[-1]
+        thirds = jnp.concatenate(thirds, axis=0).T.astype(BF16)
+        for n in range(COLS // SPREAD):
+            cols = slice(n * SPREAD, (n + 1) * SPREAD)
+            wide = jnp.dot(thirds, select[:, cols], preferred_element_type=F32)
+            v = held[c % STAGES, :, cols].astype(F32) * wide
+            slab[rows, cols] = v.astype(BF16)
+
+        @pl.when(c + STAGES < STEPS)
+        def _():
+            code_copy(c + STAGES).start()
+
         r = jnp.dot(slab[rows, :], pext[...], preferred_element_type=F32)
         part[rows, :] = r[:, :K]
         for t in range(CHUNK // 128):
@@ -200,13 +235,16 @@
             for j in (2, 1, 3):
                 send(tilt.at[mine], tilt.at[mine], send_sem.at[3, h, slot], recv_sem.at[3, h, c], a_peer(j))
 
-    def stage_e(c):
+    def tilted_at(c):
         slot = c % (LAG + 1)
         for h in range(2):
             wait_for(tilt.at[pl.ds(0, 3 * PA)], recv_sem.at[3, h, c])
             wait_for(tilt.at[pl.ds(0, 3 * PA)], send_sem.at[3, h, slot])
+        return tilt[rows_at(c, 0, CHUNK), :].T.astype(BF16)
+
+    def stage_e(c):
+        t = tilted_at(c)
         rows = rows_at(c, 0, CHUNK)
-        t = tilt[rows, :].T.astype(BF16)
         for p in range(8):
             acc[p] += jnp.dot(t, slab[rows, p * 256 : (p + 1) * 256], preferred_element_type=F32)
 
@@ -215,9 +253,8 @@
             own_p[...], own_t[...], (((0,), (0,)), ((), ())),
             precision=HI, preferred_element_type=F32,
         )
-        probes = pext[:, :K]
         selfg = lax.dot_general(
-            probes, probes, (((0,), (0,)), ((), ())), preferred_element_type=F32
+            probes[...], probes[...], (((0,), (0,)), ((), ())), preferred_element_type=F32
         ) * 0.125
         for i in range(16):
             gsend[i, :8] = cross[i * 8 : (i + 1) * 8]
@@ -245,11 +282,24 @@
         at_lag(4, stage_e)
         return 0
 
-    lax.fori_loop(0, STEPS + 4 * LAG, tick, 0)
-
-    theirs = pl.ds((1 - core) * 4, 4)
-    ours = core * 4
-    send(acc.at[theirs], rc, tsend.at[1], trecv.at[1], core_peer)
+    lax.fori_loop(0, STEPS + 4 * LAG - 1, tick, 0)
+
+    theirs, ours = (1 - core) * 4, core * 4
+    last = tilted_at(STEPS - 1)
+    rows = rows_at(STEPS - 1, 0, CHUNK)
+
+    def add_last(p):
+        cols = pl.ds(pl.multiple_of(p * 256, 256), 256)
+        acc[p] += jnp.dot(last, slab[rows, cols], preferred_element_type=F32)
+
+    for i in range(4):
+        add_last(theirs + i)
+        send(acc.at[theirs + i], rc.at[i], csend.at[i], crecv.at[i], core_peer)
+    for i in range(4):
+        add_last(ours + i)
+    for i in range(16):
+        block = probes[i * 128 : (i + 1) * 128, :].astype(F32).T
+        probes_t[i // 2, :, (i % 2) * 128 : (i % 2 + 1) * 128] = block
 
     wait_for(g1.at[pl.ds(0, 15)], trecv.at[0])
     wait_for(g1.at[pl.ds(0, 15)], tsend.at[0])
@@ -261,12 +311,13 @@
     for j in range(1, 8):
         send(g3.at[d], g3.at[d], tsend.at[2], trecv.at[2], dp_peer(j))
 
-    wait_for(rc, trecv.at[1])
-    wait_for(rc, tsend.at[1])
-    for i in range(4):
+    for j in (2, 1, 3, 0):
+        i = (z + j) % 4
+        wait_for(rc.at[i], crecv.at[i])
+        wait_for(rc.at[i], csend.at[i])
         rc[i] = rc[i] + acc[ours + i]
-    for j in (2, 1, 3):
-        send(rc.at[(z + j) % 4], rz.at[j - 1], tsend.at[3], trecv.at[3], z_peer(j))
+        if j:
+            send(rc.at[i], rz.at[j - 1], tsend.at[3], trecv.at[3], z_peer(j))
 
     wait_for(g3.at[pl.ds(0, 7)], trecv.at[2])
     wait_for(g3.at[pl.ds(0, 7)], tsend.at[2])
@@ -318,33 +369,29 @@
     gram = cross + shift * selfg
     gram = 0.5 * (gram + gram.T)
     lower_inverse(gmat, wmat, gram)
-    inv = wmat[pl.ds(pl.multiple_of(d * 16, 8), 16), :] * (float(F) ** 0.5)
-    from_probes = lax.dot_general(
-        inv, pext[:, :K].astype(F32), (((1,), (1,)), ((), ())),
-        precision=HI, preferred_element_type=F32,
-    )
+    inv = wmat[pl.ds(pl.multiple_of(d * 16, 8), 16), :]
 
     wait_for(full.at[pl.ds(0, 4)], trecv.at[8])
     wait_for(full.at[pl.ds(0, 4)], tsend.at[8])
     for p in range(8):
-        cols = slice(p * 256, (p + 1) * 256)
-        out[:, cols] = shift * from_probes[:, cols] + jnp.dot(
-            inv, full[p], precision=HI, preferred_element_type=F32
+        out[:, p * 256 : (p + 1) * 256] = jnp.dot(
+            inv, full[p] + shift * probes_t[p], precision=HI, preferred_element_type=F32
         )
 
 
 def body(codes, scales, logit_weight, probes):
-    pext = jnp.concatenate(
-        [probes, jnp.broadcast_to(logit_weight[:, None], (COLS, K))], axis=1
-    )
     vmem = pl.BlockSpec(memory_space=pltpu.VMEM)
     dma = pltpu.SemaphoreType.DMA
     result = pl.pallas_call(
         kernel,
         out_shape=jax.ShapeDtypeStruct((16, COLS), F32),
-        in_specs=[pl.BlockSpec(memory_space=pl.ANY), vmem, vmem],
+        in_specs=[pl.BlockSpec(memory_space=pl.ANY), vmem, vmem, vmem],
         out_specs=vmem,
         scratch_shapes=[
+            pltpu.VMEM((COLS, 2 * K), BF16),
+            pltpu.VMEM((3 * BLOCKS, COLS), BF16),
+            pltpu.VMEM((8, K, 256), F32),
+            pltpu.VMEM((STAGES, CHUNK, COLS), BF16),
             pltpu.VMEM((ROWS, COLS), BF16),
             pltpu.VMEM((ROWS, K), F32),
             pltpu.VMEM((2, STEPS, 3, PA, K), F32),
@@ -368,20 +415,22 @@
             pltpu.VMEM((16, 8, K), F32),
             pltpu.VMEM((K, K), F32),
             pltpu.VMEM((K, K), F32),
-            dma((STEPS,)),
+            dma((STAGES,)),
             dma((4, 2, LAG + 1)),
             dma((4, 2, STEPS)),
             dma((2, LAG + 1)),
             dma((2, STEPS)),
             dma((9,)),
             dma((9,)),
+            dma((4,)),
+            dma((4,)),
         ],
         compiler_params=pltpu.CompilerParams(
             collective_id=0, has_side_effects=True, vmem_limit_bytes=58 << 20
         ),
         name="sketch",
-    )(codes, scales, pext)
-    return result.T
+    )(codes, scales, logit_weight.reshape(BLOCKS, QB), probes)
+    return result.T * jnp.sqrt(F32(F))
 
 
 def solution(mesh):

time: 106 us -> 85.5 us (0.81)
  Pallas kernels: 101 us -> 83.8 us
  local copies, waits for them, and re-layouts: 2.59 us -> 0 us
    pallas_call x1, Pallas kernels: 101 us -> 83.8 us  [body(): pl.pallas_call(kernel, out_shape=jax.ShapeDtypeStruct((16, COLS), F32), i...]
    concatenate x1 -> x0, other arithmetic: 2.15 us -> none  [body(): jnp.concatenate([probes, jnp.broadcast_to(logit_weight[:, None], (COLS, K...]
    mul x0 -> x1, other arithmetic: none -> 1.57 us  [body(): return result.T * jnp.sqrt(F32(F))]
    unnamed x1 -> x0, local copies, waits for them, and re-layouts: 1.57 us -> none
where the time goes in v2:
time: 85.5 us; the launch traced here: 85.3 us
  Pallas kernels  83.8 us (98%)
  other arithmetic  1.57 us (2%)
    pallas_call x1, Pallas kernels, body(): pl.pallas_call(kernel, out_shape=jax.ShapeDtypeStruct((16, COLS), F32), i...  83.8 us

profile of v2, /device:TPU:1, one launch (start us, length us, event | category | flops | bytes accessed | tf_op | source)
XLA Modules:
  0.0 85.3 jit_solution(6309073820602742893)
XLA Ops:
  0.0 83.8 %sketch.1 = f32[16,2048]{1,0:T(8,128)} custom-call(bf16[5632,2048]{1,0:T(8,128)(2,1)} %codes.1, f32[16,5632]{1,0:T(8,128)} %scales.1, bf16[16,128]{1,0:T(8,128)(2,1)} %bitcast.3, bf16[2048,128]{1,0:T(8,128)(2,1)} %probes.1), custom_call_target="tpu_custom_call" | custom-call | tf_op jit(solution)/shard_map/sketch/pallas_call | solution.py:385
  83.8 1.6 %multiply_bitcast_fusion = f32[2048,16]{0,1:T(8,128)} fusion(f32[16,2048]{1,0:T(8,128)} %sketch.1), kind=kLoop, calls=%fused_computation | loop fusion | flops 32768 | bytes 262144 | tf_op jit(solution)/shard_map/mul | solution.py:433

commit v3 on v2

--- a/solution.py
+++ b/solution.py
@@ -15,11 +15,13 @@
 BLOCKS = COLS // QB
 CHUNK = 512
 STEPS = ROWS // CHUNK
-LAG = 3
+LAGS = (0, 3, 6, 9, 12)
+LAG = max(LAGS[i + 1] - LAGS[i] for i in range(4))
 HALF = CHUNK // 2
 PA = HALF // 4
 PB = PA // 4
 SPREAD = 256
+SECTION = 32
 PANEL = 4
 STAGES = 3
 MESH = pl.DeviceIdType.MESH
@@ -39,14 +41,14 @@
     w_ref[...] = jnp.where(sub == lane, 1.0, 0.0).astype(F32)
     lane_row, sub_col = lane[:1], sub[:, :1]
 
-    def step(i, _):
+    def step(top, i, _):
         first = i * PANEL
-        a = g_ref[...]
-        w = w_ref[...]
+        a = g_ref[top:, :]
+        w = w_ref[top:, :]
         row_a = [g_ref[pl.ds(first + j, 1), :] for j in range(PANEL)]
         row_w = [w_ref[pl.ds(first + j, 1), :] for j in range(PANEL)]
         col = [
-            jnp.sum(jnp.where(lane == first + j, a, 0.0), axis=1, keepdims=True)
+            jnp.sum(jnp.where(lane[top:] == first + j, a, 0.0), axis=1, keepdims=True)
             for j in range(PANEL)
         ]
         corner = {
@@ -65,14 +67,15 @@
                 col[j] = col[j] - ratio * col[m]
                 for q in range(j, PANEL):
                     corner[j, q] = corner[j, q] - ratio * corner[m, q]
-            factor = jnp.where(sub_col > first + m, col[m] * inverse, 0.0)
+            factor = jnp.where(sub_col[top:] > first + m, col[m] * inverse, 0.0)
             a = a - factor * row_a[m]
             w = w - factor * row_w[m]
-        g_ref[...] = a
-        w_ref[...] = w
+        g_ref[top:, :] = a
+        w_ref[top:, :] = w
         return 0
 
-    lax.fori_loop(0, K // PANEL, step, 0)
+    for top in range(0, K, SECTION):
+        lax.fori_loop(top // PANEL, (top + SECTION) // PANEL, functools.partial(step, top), 0)
     diag = jnp.sum(jnp.where(sub == lane, g_ref[...], 0.0), axis=1, keepdims=True)
     w_ref[...] = w_ref[...] * lax.rsqrt(diag)
 
@@ -128,7 +131,6 @@
     for b in range(BLOCKS):
         row = weight[...].astype(F32)[b : b + 1]
         pext[b * QB : (b + 1) * QB, K:] = jnp.broadcast_to(row, (K, QB)).T.astype(BF16)
-    pl.semaphore_wait(barrier, 22)
 
     axes = ((x, y, x_peer, y_peer), (y, x, y_peer, x_peer))
 
@@ -143,8 +145,7 @@
         jnp.int32, (K, K), 1
     )
 
-    def stage_a(c):
-        slot = c % (LAG + 1)
+    def project(c):
         code_copy(c).wait()
 
         rows = rows_at(c, 0, CHUNK)
@@ -171,6 +172,8 @@
                 jnp.where(eye, r[t * 128 : (t + 1) * 128, K:], 0.0),
                 axis=0, keepdims=True,
             )
+    def stage_a(c):
+        slot = c % (LAG + 1)
         for j in range(1, 4):
             send(lg.at[c], lx.at[c, j - 1], lsend_sem.at[0, slot], lrecv_sem.at[0, c], x_peer(j))
         for h in range(2):
@@ -211,10 +214,10 @@
             wait_for(rb.at[h, c], send_sem.at[1, h, slot])
             at = pl.ds(pl.multiple_of(pb * PB, 8), PB)
             p = sa[h, c, at, :] + rb[h, c, 0] + rb[h, c, 1] + rb[h, c, 2]
-            curv = lg[c, pl.ds(h * 2 + pa // 2, 1), :]
-            first = (pa % 2) * PA + pb * PB
+            first = h * HALF + pa * PA + pb * PB
+            curv = lg[c, pl.ds(first // K, 1), :]
             column = jnp.sum(
-                jnp.where(lane == sub + first, curv, 0.0), axis=1, keepdims=True
+                jnp.where(lane == sub + first % K, curv, 0.0), axis=1, keepdims=True
             )
             t = (column * p).astype(BF16).astype(F32)
             mine = rows_at(c, h * HALF + pa * PA + pb * PB, PB)
@@ -264,25 +267,27 @@
 
     def tick(t, _):
         def at_lag(n, stage):
-            c = t - n * LAG
+            c = t - LAGS[n]
 
             @pl.when((c >= 0) & (c < STEPS))
             def _():
                 stage(c)
 
+        at_lag(0, stage_a)
+        at_lag(1, stage_b)
+        at_lag(2, stage_c)
         at_lag(3, stage_d)
-        at_lag(2, stage_c)
-        at_lag(1, stage_b)
-        at_lag(0, stage_a)
-
-        @pl.when(t == STEPS + 2 * LAG)
+
+        @pl.when(t + 1 < STEPS)
         def _():
-            gram_out()
+            project(t + 1)
 
         at_lag(4, stage_e)
         return 0
 
-    lax.fori_loop(0, STEPS + 4 * LAG - 1, tick, 0)
+    project(0)
+    pl.semaphore_wait(barrier, 22)
+    lax.fori_loop(0, STEPS + LAGS[4] - 1, tick, 0)
 
     theirs, ours = (1 - core) * 4, core * 4
     last = tilted_at(STEPS - 1)
@@ -297,6 +302,16 @@
         send(acc.at[theirs + i], rc.at[i], csend.at[i], crecv.at[i], core_peer)
     for i in range(4):
         add_last(ours + i)
+
+    for j in (2, 1, 3, 0):
+        i = (z + j) % 4
+        wait_for(rc.at[i], crecv.at[i])
+        wait_for(rc.at[i], csend.at[i])
+        rc[i] = rc[i] + acc[ours + i]
+        if j:
+            send(rc.at[i], rz.at[j - 1], tsend.at[3], trecv.at[3], z_peer(j))
+
+    gram_out()
     for i in range(16):
         block = probes[i * 128 : (i + 1) * 128, :].astype(F32).T
         probes_t[i // 2, :, (i % 2) * 128 : (i % 2 + 1) * 128] = block
@@ -310,23 +325,6 @@
     g3[d] = g
     for j in range(1, 8):
         send(g3.at[d], g3.at[d], tsend.at[2], trecv.at[2], dp_peer(j))
-
-    for j in (2, 1, 3, 0):
-        i = (z + j) % 4
-        wait_for(rc.at[i], crecv.at[i])
-        wait_for(rc.at[i], csend.at[i])
-        rc[i] = rc[i] + acc[ours + i]
-        if j:
-            send(rc.at[i], rz.at[j - 1], tsend.at[3], trecv.at[3], z_peer(j))
-
-    wait_for(g3.at[pl.ds(0, 7)], trecv.at[2])
-    wait_for(g3.at[pl.ds(0, 7)], tsend.at[2])
-    g = g3[0]
-    for i in range(1, 8):
-        g = g + g3[i]
-    gf[f] = g
-    for j in range(1, 16):
-        send(gf.at[f], gf.at[f], tsend.at[4], trecv.at[4], plane_peer(j))
 
     wait_for(rz, trecv.at[3])
     wait_for(rz, tsend.at[3])
@@ -338,6 +336,16 @@
     sq1[d] = sq[:, :128] + sq[:, 128:]
     for j in range(1, 8):
         send(sq1.at[d], sq1.at[d], tsend.at[5], trecv.at[5], dp_peer(j))
+
+    wait_for(g3.at[pl.ds(0, 7)], trecv.at[2])
+    wait_for(g3.at[pl.ds(0, 7)], tsend.at[2])
+    g = g3[0]
+    for i in range(1, 8):
+        g = g + g3[i]
+    gf[f] = g
+    for j in range(1, 16):
+        send(gf.at[f], gf.at[f], tsend.at[4], trecv.at[4], plane_peer(j))
+
     for j in (2, 1, 3):
         send(full.at[mine], full.at[mine], tsend.at[6], trecv.at[6], z_peer(j))
 
@@ -426,7 +434,7 @@
             dma((4,)),
         ],
         compiler_params=pltpu.CompilerParams(
-            collective_id=0, has_side_effects=True, vmem_limit_bytes=58 << 20
+            collective_id=0, has_side_effects=True, vmem_limit_bytes=48 << 20
         ),
         name="sketch",
     )(codes, scales, logit_weight.reshape(BLOCKS, QB), probes)

time: 85.5 us -> 81.5 us (0.953)
  Pallas kernels: 83.8 us -> 77.9 us
  local copies, waits for them, and re-layouts: 0 us -> 2.71 us
  other arithmetic: 1.57 us -> 0.67 us
    pallas_call x1, Pallas kernels: 83.8 us -> 77.9 us  [body(): pl.pallas_call(kernel, out_shape=jax.ShapeDtypeStruct((16, COLS), F32), i...]
    unnamed x0 -> x6, local copies, waits for them, and re-layouts: none -> 2.71 us
    mul x1, other arithmetic: 1.57 us -> 0.67 us  [body(): return result.T * jnp.sqrt(F32(F))]
where the time goes in v3:
time: 81.5 us; the launch traced here: 81.3 us
  Pallas kernels  77.9 us (96%)
  local copies, waits for them, and re-layouts  2.71 us (3%)
    pallas_call x1, Pallas kernels, body(): pl.pallas_call(kernel, out_shape=jax.ShapeDtypeStruct((16, COLS), F32), i...  77.9 us
    unnamed x6, local copies, waits for them, and re-layouts  2.71 us

profile of v3, /device:TPU:1, one launch (start us, length us, event | category | flops | bytes accessed | tf_op | source)
XLA Modules:
  0.0 81.3 jit_solution(8199270165878247302)
XLA Ops:
  0.0 0.0 copy-start
  0.0 1.0 %copy-done = bf16[2048,128]{1,0:T(8,128)(2,1)S(1)} copy-done((bf16[2048,128]{1,0:T(8,128)(2,1)S(1)}, bf16[2048,128]{1,0:T(8,128)(2,1)}, u32[]{:S(2)}) %copy-start) | copy-done | bytes 524312
  1.0 0.0 copy-start.1
  1.0 1.0 %copy-done.1 = f32[16,5632]{1,0:T(8,128)S(1)} copy-done((f32[16,5632]{1,0:T(8,128)S(1)}, f32[16,5632]{1,0:T(8,128)}, u32[]{:S(2)}) %copy-start.1) | copy-done | bytes 360472
  2.0 0.0 copy-start.2
  2.0 0.7 copy-done.2
  2.7 77.9 %sketch.1 = f32[16,2048]{1,0:T(8,128)S(1)} custom-call(bf16[5632,2048]{1,0:T(8,128)(2,1)} %codes.1, f32[16,5632]{1,0:T(8,128)S(1)} %copy-done.1, bf16[16,128]{1,0:T(8,128)(2,1)S(1)} %bitcast.3, bf16[2048,128]{1,0:T(8,128)(2,1)S(1)} %copy-done), custom_call_target="tpu_custom_call" | custom-call | tf_op jit(solution)/shard_map/sketch/pallas_call | solution.py:393
  80.6 0.7 multiply_bitcast_fusion
Async XLA Ops:
  0.0 1.0 %copy-start = (bf16[2048,128]{1,0:T(8,128)(2,1)S(1)}, bf16[2048,128]{1,0:T(8,128)(2,1)}, u32[]{:S(2)}) copy-start(bf16[2048,128]{1,0:T(8,128)(2,1)} %probes.1) | copy-start | bytes 1572868
  1.0 1.0 %copy-start.1 = (f32[16,5632]{1,0:T(8,128)S(1)}, f32[16,5632]{1,0:T(8,128)}, u32[]{:S(2)}) copy-start(f32[16,5632]{1,0:T(8,128)} %scales.1) | copy-start | bytes 1081348
  2.0 0.7 copy-start.2

commit v4 on v3

--- a/solution.py
+++ b/solution.py
@@ -21,7 +21,7 @@
 PA = HALF // 4
 PB = PA // 4
 SPREAD = 256
-SECTION = 32
+SECTION = 16
 PANEL = 4
 STAGES = 3
 MESH = pl.DeviceIdType.MESH
@@ -34,7 +34,7 @@
     pltpu.make_async_copy(ref, ref, sem).wait()
 
 
-def lower_inverse(g_ref, w_ref, gram):
+def lower_inverse(g_ref, w_ref, gram, halfway):
     sub = lax.broadcasted_iota(jnp.int32, (K, K), 0)
     lane = lax.broadcasted_iota(jnp.int32, (K, K), 1)
     g_ref[...] = gram
@@ -75,17 +75,19 @@
         return 0
 
     for top in range(0, K, SECTION):
+        if top == K // 2:
+            halfway()
         lax.fori_loop(top // PANEL, (top + SECTION) // PANEL, functools.partial(step, top), 0)
     diag = jnp.sum(jnp.where(sub == lane, g_ref[...], 0.0), axis=1, keepdims=True)
     w_ref[...] = w_ref[...] * lax.rsqrt(diag)
 
 
 def kernel(
-    codes, scales, weight, probes, out,
-    pext, select, probes_t, held, slab, part, ra, sa, rb, tilt, own_p, own_t,
+    codes, scales_in, weight_in, probes_in, out,
+    scales, weight, probes, pext, select, probes_t, held, slab, part, ra, sa, rb, tilt, own_p, own_t,
     lg, lx, ly, acc, rc, rz, full,
     gsend, g1, g3, gf, sq1, sq2, gmat, wmat,
-    code_sem, send_sem, recv_sem, lsend_sem, lrecv_sem, tsend, trecv, csend, crecv,
+    code_sem, send_sem, recv_sem, lsend_sem, lrecv_sem, tsend, trecv, csend, crecv, in_sem,
 ):
     d = lax.axis_index("dp")
     f = lax.axis_index("feat")
@@ -100,8 +102,15 @@
             codes.at[rows_at(c, 0, CHUNK)], held.at[c % STAGES], code_sem.at[c % STAGES]
         )
 
-    for c in range(STAGES):
-        code_copy(c).start()
+    inputs = [
+        pltpu.make_async_copy(src, dst, in_sem.at[i])
+        for i, (src, dst) in enumerate(
+            ((probes_in, probes), (weight_in, weight), (scales_in, scales))
+        )
+    ]
+    for copy in inputs:
+        copy.start()
+    code_copy(0).start()
 
     def x_peer(j):
         return (d, y * 4 + (x + j) % 4)
@@ -124,6 +133,8 @@
         pl.semaphore_signal(barrier, 1, device_id=plane_peer(j), device_id_type=MESH)
     for j in range(1, 8):
         pl.semaphore_signal(barrier, 1, device_id=dp_peer(j), device_id_type=MESH)
+    for copy in inputs:
+        copy.wait()
     pext[:, :K] = probes[...]
     block = lax.broadcasted_iota(jnp.int32, (3 * BLOCKS, COLS), 0) % BLOCKS
     lane_block = lax.broadcasted_iota(jnp.int32, (3 * BLOCKS, COLS), 1) // QB
@@ -178,7 +189,7 @@
             send(lg.at[c], lx.at[c, j - 1], lsend_sem.at[0, slot], lrecv_sem.at[0, c], x_peer(j))
         for h in range(2):
             pa, pb, a_peer, b_peer = axes[h]
-            for j in (2, 1, 3):
+            for j in (1, 3, 2):
                 at = rows_at(c, h * HALF + ((pa + j) % 4) * PA, PA)
                 send(part.at[at], ra.at[h, c, j - 1], send_sem.at[0, h, slot], recv_sem.at[0, h, c], a_peer(j))
 
@@ -195,7 +206,7 @@
             wait_for(ra.at[h, c], send_sem.at[0, h, slot])
             at = rows_at(c, h * HALF + pa * PA, PA)
             sa[h, c] = part[at, :] + ra[h, c, 0] + ra[h, c, 1] + ra[h, c, 2]
-            for j in (2, 1, 3):
+            for j in (1, 3, 2):
                 at = pl.ds(pl.multiple_of(((pb + j) % 4) * PB, 8), PB)
                 send(sa.at[h, c, at], rb.at[h, c, j - 1], send_sem.at[1, h, slot], recv_sem.at[1, h, c], b_peer(j))
 
@@ -225,7 +236,7 @@
             keep = pl.ds(pl.multiple_of((c * 2 + h) * PB, 8), PB)
             own_p[keep, :] = p
             own_t[keep, :] = t
-            for j in (2, 1, 3):
+            for j in (1, 3, 2):
                 send(tilt.at[mine], tilt.at[mine], send_sem.at[2, h, slot], recv_sem.at[2, h, c], b_peer(j))
 
     def stage_d(c):
@@ -235,7 +246,7 @@
             wait_for(tilt.at[pl.ds(0, 3 * PB)], recv_sem.at[2, h, c])
             wait_for(tilt.at[pl.ds(0, 3 * PB)], send_sem.at[2, h, slot])
             mine = rows_at(c, h * HALF + pa * PA, PA)
-            for j in (2, 1, 3):
+            for j in (1, 3, 2):
                 send(tilt.at[mine], tilt.at[mine], send_sem.at[3, h, slot], recv_sem.at[3, h, c], a_peer(j))
 
     def tilted_at(c):
@@ -285,6 +296,8 @@
         at_lag(4, stage_e)
         return 0
 
+    for c in range(1, STAGES):
+        code_copy(c).start()
     project(0)
     pl.semaphore_wait(barrier, 22)
     lax.fori_loop(0, STEPS + LAGS[4] - 1, tick, 0)
@@ -297,7 +310,8 @@
         cols = pl.ds(pl.multiple_of(p * 256, 256), 256)
         acc[p] += jnp.dot(last, slab[rows, cols], preferred_element_type=F32)
 
-    for i in range(4):
+    for j in (2, 1, 3, 0):
+        i = (z + j) % 4
         add_last(theirs + i)
         send(acc.at[theirs + i], rc.at[i], csend.at[i], crecv.at[i], core_peer)
     for i in range(4):
@@ -336,6 +350,8 @@
     sq1[d] = sq[:, :128] + sq[:, 128:]
     for j in range(1, 8):
         send(sq1.at[d], sq1.at[d], tsend.at[5], trecv.at[5], dp_peer(j))
+    for j in (1, 3, 2):
+        send(full.at[mine], full.at[mine], tsend.at[6], trecv.at[6], z_peer(j))
 
     wait_for(g3.at[pl.ds(0, 7)], trecv.at[2])
     wait_for(g3.at[pl.ds(0, 7)], tsend.at[2])
@@ -346,8 +362,6 @@
     for j in range(1, 16):
         send(gf.at[f], gf.at[f], tsend.at[4], trecv.at[4], plane_peer(j))
 
-    for j in (2, 1, 3):
-        send(full.at[mine], full.at[mine], tsend.at[6], trecv.at[6], z_peer(j))
 
     wait_for(sq1.at[pl.ds(0, 7)], trecv.at[5])
     wait_for(sq1.at[pl.ds(0, 7)], tsend.at[5])
@@ -357,10 +371,6 @@
     sq2[f] = sq
     for j in range(1, 16):
         send(sq2.at[f], sq2.at[f], tsend.at[7], trecv.at[7], plane_peer(j))
-
-    wait_for(full.at[pl.ds(0, 3)], trecv.at[6])
-    wait_for(full.at[pl.ds(0, 3)], tsend.at[6])
-    send(full.at[pl.ds(ours, 4)], full.at[pl.ds(ours, 4)], tsend.at[8], trecv.at[8], core_peer)
 
     wait_for(gf.at[pl.ds(0, 15)], trecv.at[4])
     wait_for(gf.at[pl.ds(0, 15)], tsend.at[4])
@@ -376,7 +386,14 @@
     shift = 0.1 * jnp.sqrt(total / (F * K))
     gram = cross + shift * selfg
     gram = 0.5 * (gram + gram.T)
-    lower_inverse(gmat, wmat, gram)
+
+    def pass_on():
+        wait_for(full.at[pl.ds(0, 3)], trecv.at[6])
+        wait_for(full.at[pl.ds(0, 3)], tsend.at[6])
+        half = full.at[pl.ds(ours, 4)]
+        send(half, half, tsend.at[8], trecv.at[8], core_peer)
+
+    lower_inverse(gmat, wmat, gram, pass_on)
     inv = wmat[pl.ds(pl.multiple_of(d * 16, 8), 16), :]
 
     wait_for(full.at[pl.ds(0, 4)], trecv.at[8])
@@ -393,9 +410,12 @@
     result = pl.pallas_call(
         kernel,
         out_shape=jax.ShapeDtypeStruct((16, COLS), F32),
-        in_specs=[pl.BlockSpec(memory_space=pl.ANY), vmem, vmem, vmem],
+        in_specs=[pl.BlockSpec(memory_space=pl.ANY)] * 4,
         out_specs=vmem,
         scratch_shapes=[
+            pltpu.VMEM((BLOCKS, ROWS), F32),
+            pltpu.VMEM((BLOCKS, QB), BF16),
+            pltpu.VMEM((COLS, K), BF16),
             pltpu.VMEM((COLS, 2 * K), BF16),
             pltpu.VMEM((3 * BLOCKS, COLS), BF16),
             pltpu.VMEM((8, K, 256), F32),
@@ -432,6 +452,7 @@
             dma((9,)),
             dma((4,)),
             dma((4,)),
+            dma((3,)),
         ],
         compiler_params=pltpu.CompilerParams(
             collective_id=0, has_side_effects=True, vmem_limit_bytes=48 << 20

time: 81.5 us -> 80.7 us (level)
    pallas_call x1, Pallas kernels: 77.9 us -> 77.1 us  [body(): pl.pallas_call(kernel, out_shape=jax.ShapeDtypeStruct((16, COLS), F32), i...]
where the time goes in v4:
time: 80.7 us; the launch traced here: 80.5 us
  Pallas kernels  77.1 us (96%)
  local copies, waits for them, and re-layouts  2.71 us (3%)
    pallas_call x1, Pallas kernels, body(): pl.pallas_call(kernel, out_shape=jax.ShapeDtypeStruct((16, COLS), F32), i...  77.1 us
    unnamed x6, local copies, waits for them, and re-layouts  2.71 us

profile of v4, /device:TPU:1, one launch (start us, length us, event | category | flops | bytes accessed | tf_op | source)
XLA Modules:
  0.0 80.5 jit_solution(10795533213037739737)
XLA Ops:
  0.0 0.0 copy-start
  0.0 1.0 %copy-done = bf16[2048,128]{1,0:T(8,128)(2,1)S(1)} copy-done((bf16[2048,128]{1,0:T(8,128)(2,1)S(1)}, bf16[2048,128]{1,0:T(8,128)(2,1)}, u32[]{:S(2)}) %copy-start) | copy-done | bytes 524312
  1.0 0.0 copy-start.1
  1.0 1.0 %copy-done.1 = f32[16,5632]{1,0:T(8,128)S(1)} copy-done((f32[16,5632]{1,0:T(8,128)S(1)}, f32[16,5632]{1,0:T(8,128)}, u32[]{:S(2)}) %copy-start.1) | copy-done | bytes 360472
  2.0 0.0 copy-start.2
  2.0 0.7 copy-done.2
  2.7 77.1 %sketch.1 = f32[16,2048]{1,0:T(8,128)S(1)} custom-call(bf16[5632,2048]{1,0:T(8,128)(2,1)} %codes.1, f32[16,5632]{1,0:T(8,128)S(1)} %copy-done.1, bf16[16,128]{1,0:T(8,128)(2,1)S(1)} %bitcast.3, bf16[2048,128]{1,0:T(8,128)(2,1)S(1)} %copy-done), custom_call_target="tpu_custom_call" | custom-call | tf_op jit(solution)/shard_map/sketch/pallas_call | solution.py:410
  79.8 0.7 multiply_bitcast_fusion
Async XLA Ops:
  0.0 1.0 %copy-start = (bf16[2048,128]{1,0:T(8,128)(2,1)S(1)}, bf16[2048,128]{1,0:T(8,128)(2,1)}, u32[]{:S(2)}) copy-start(bf16[2048,128]{1,0:T(8,128)(2,1)} %probes_in.1) | copy-start | bytes 1572868
  1.0 1.0 %copy-start.1 = (f32[16,5632]{1,0:T(8,128)S(1)}, f32[16,5632]{1,0:T(8,128)}, u32[]{:S(2)}) copy-start(f32[16,5632]{1,0:T(8,128)} %scales_in.1) | copy-start | bytes 1081348
  2.0 0.7 copy-start.2

commit v5 on v4

--- a/solution.py
+++ b/solution.py
@@ -320,7 +320,6 @@
     for j in (2, 1, 3, 0):
         i = (z + j) % 4
         wait_for(rc.at[i], crecv.at[i])
-        wait_for(rc.at[i], csend.at[i])
         rc[i] = rc[i] + acc[ours + i]
         if j:
             send(rc.at[i], rz.at[j - 1], tsend.at[3], trecv.at[3], z_peer(j))
@@ -331,7 +330,6 @@
         probes_t[i // 2, :, (i % 2) * 128 : (i % 2 + 1) * 128] = block
 
     wait_for(g1.at[pl.ds(0, 15)], trecv.at[0])
-    wait_for(g1.at[pl.ds(0, 15)], tsend.at[0])
     g1[f] = gsend[f]
     g = g1[0]
     for i in range(1, 16):
@@ -341,7 +339,6 @@
         send(g3.at[d], g3.at[d], tsend.at[2], trecv.at[2], dp_peer(j))
 
     wait_for(rz, trecv.at[3])
-    wait_for(rz, tsend.at[3])
     s = rc[z] + rz[0] + rz[1] + rz[2]
     mine = ours + z
     full[mine] = s
@@ -354,7 +351,6 @@
         send(full.at[mine], full.at[mine], tsend.at[6], trecv.at[6], z_peer(j))
 
     wait_for(g3.at[pl.ds(0, 7)], trecv.at[2])
-    wait_for(g3.at[pl.ds(0, 7)], tsend.at[2])
     g = g3[0]
     for i in range(1, 8):
         g = g + g3[i]
@@ -364,7 +360,6 @@
 
 
     wait_for(sq1.at[pl.ds(0, 7)], trecv.at[5])
-    wait_for(sq1.at[pl.ds(0, 7)], tsend.at[5])
     sq = sq1[0]
     for i in range(1, 8):
         sq = sq + sq1[i]
@@ -373,12 +368,10 @@
         send(sq2.at[f], sq2.at[f], tsend.at[7], trecv.at[7], plane_peer(j))
 
     wait_for(gf.at[pl.ds(0, 15)], trecv.at[4])
-    wait_for(gf.at[pl.ds(0, 15)], tsend.at[4])
     cross = jnp.concatenate([gf[i, :8] for i in range(16)], axis=0)
     selfg = jnp.concatenate([gf[i, 8:] for i in range(16)], axis=0)
 
     wait_for(sq2.at[pl.ds(0, 15)], trecv.at[7])
-    wait_for(sq2.at[pl.ds(0, 15)], tsend.at[7])
     sq = sq2[0]
     for i in range(1, 16):
         sq = sq + sq2[i]
@@ -389,7 +382,6 @@
 
     def pass_on():
         wait_for(full.at[pl.ds(0, 3)], trecv.at[6])
-        wait_for(full.at[pl.ds(0, 3)], tsend.at[6])
         half = full.at[pl.ds(ours, 4)]
         send(half, half, tsend.at[8], trecv.at[8], core_peer)
 
@@ -397,11 +389,21 @@
     inv = wmat[pl.ds(pl.multiple_of(d * 16, 8), 16), :]
 
     wait_for(full.at[pl.ds(0, 4)], trecv.at[8])
-    wait_for(full.at[pl.ds(0, 4)], tsend.at[8])
     for p in range(8):
         out[:, p * 256 : (p + 1) * 256] = jnp.dot(
             inv, full[p] + shift * probes_t[p], precision=HI, preferred_element_type=F32
         )
+
+    for i in range(4):
+        wait_for(rc.at[i], csend.at[i])
+    wait_for(g1.at[pl.ds(0, 15)], tsend.at[0])
+    wait_for(rz, tsend.at[3])
+    wait_for(g3.at[pl.ds(0, 7)], tsend.at[2])
+    wait_for(sq1.at[pl.ds(0, 7)], tsend.at[5])
+    wait_for(gf.at[pl.ds(0, 15)], tsend.at[4])
+    wait_for(sq2.at[pl.ds(0, 15)], tsend.at[7])
+    wait_for(full.at[pl.ds(0, 3)], tsend.at[6])
+    wait_for(full.at[pl.ds(0, 4)], tsend.at[8])
 
 
 def body(codes, scales, logit_weight, probes):

time: 80.7 us -> 80.7 us (level)
  no operation moved by 1% of the time
where the time goes in v5:
time: 80.7 us; the launch traced here: 80.5 us
  Pallas kernels  77.1 us (96%)
  local copies, waits for them, and re-layouts  2.71 us (3%)
    pallas_call x1, Pallas kernels, body(): pl.pallas_call(kernel, out_shape=jax.ShapeDtypeStruct((16, COLS), F32), i...  77.1 us
    unnamed x6, local copies, waits for them, and re-layouts  2.71 us

profile of v5, /device:TPU:1, one launch (start us, length us, event | category | flops | bytes accessed | tf_op | source)
XLA Modules:
  0.0 80.5 jit_solution(5386460557663601730)
XLA Ops:
  0.0 0.0 copy-start
  0.0 1.0 %copy-done = bf16[2048,128]{1,0:T(8,128)(2,1)S(1)} copy-done((bf16[2048,128]{1,0:T(8,128)(2,1)S(1)}, bf16[2048,128]{1,0:T(8,128)(2,1)}, u32[]{:S(2)}) %copy-start) | copy-done | bytes 524312
  1.0 0.0 copy-start.1
  1.0 1.0 %copy-done.1 = f32[16,5632]{1,0:T(8,128)S(1)} copy-done((f32[16,5632]{1,0:T(8,128)S(1)}, f32[16,5632]{1,0:T(8,128)}, u32[]{:S(2)}) %copy-start.1) | copy-done | bytes 360472
  2.0 0.0 copy-start.2
  2.0 0.7 copy-done.2
  2.7 77.1 %sketch.1 = f32[16,2048]{1,0:T(8,128)S(1)} custom-call(bf16[5632,2048]{1,0:T(8,128)(2,1)} %codes.1, f32[16,5632]{1,0:T(8,128)S(1)} %copy-done.1, bf16[16,128]{1,0:T(8,128)(2,1)S(1)} %bitcast.3, bf16[2048,128]{1,0:T(8,128)(2,1)S(1)} %copy-done), custom_call_target="tpu_custom_call" | custom-call | tf_op jit(solution)/shard_map/sketch/pallas_call | solution.py:412
  79.8 0.7 multiply_bitcast_fusion
Async XLA Ops:
  0.0 1.0 %copy-start = (bf16[2048,128]{1,0:T(8,128)(2,1)S(1)}, bf16[2048,128]{1,0:T(8,128)(2,1)}, u32[]{:S(2)}) copy-start(bf16[2048,128]{1,0:T(8,128)(2,1)} %probes_in.1) | copy-start | bytes 1572868
  1.0 1.0 %copy-start.1 = (f32[16,5632]{1,0:T(8,128)S(1)}, f32[16,5632]{1,0:T(8,128)}, u32[]{:S(2)}) copy-start(f32[16,5632]{1,0:T(8,128)} %scales_in.1) | copy-start | bytes 1081348
  2.0 0.7 copy-start.2
